TPU v7x, 128 devices: a whole 4x4x4 slice. The times are simulated.
128 devices in a mesh: blk: 16 (over z, x_lo, core), dp: 8 (over x_hi, y).
Axes of the slice: x: 4 (x_hi: 2, x_lo: 2; x = x_hi * 2 + x_lo), y: 4, z: 4, core: 2. Of those that a mesh axis runs over, the one named last changes fastest.
Arguments:
- inputs: bfloat16 [49152, 5120], P(('blk', 'dp')), may hold values from -6 to 6
- upstream: bfloat16 [49152, 5120], P(('blk', 'dp')), may hold values from -0.625 to 0.625
- norm_gain: float32 [5120], replicated, may hold values from 0.5 to 1.5
- gate_weight: bfloat16 [5120, 7168], P('dp', 'blk'), may hold values from -0.078125 to 0.078125
- up_weight: bfloat16 [5120, 7168], P('dp', 'blk'), may hold values from -0.078125 to 0.078125
- down_weight: bfloat16 [5120, 7168], P('dp', 'blk'), may hold values from -0.25 to 0.25
Outputs:
- layer_out: bfloat16 [49152, 5120], P(('blk', 'dp'))
- grad_input: bfloat16 [49152, 5120], P(('blk', 'dp'))
- grad_gate: bfloat16 [5120, 7168], P('dp', 'blk')
- grad_up: bfloat16 [5120, 7168], P('dp', 'blk')
- grad_down: bfloat16 [5120, 7168], P('dp', 'blk')
All inputs are finite; a program needn't handle non-finite values.
Results may differ from a plain program's by a relative error of at most 0.015.
Values may be sent and summed in bfloat16 or wider, within the bound.
A program may use at most 128 MiB of HBM per device.

v0:
```python
import jax
import jax.numpy as jnp
from jax import lax
from jax.sharding import PartitionSpec as P

norm_eps = 1e-05


def shifted(value, axis, by):
    size = lax.axis_size(axis)
    return lax.ppermute(value, axis, [(i, (i + by) % size) for i in range(size)])


def contract_last(left_rows, right_rows):
    return lax.dot_general(
        left_rows, right_rows, (((1,), (1,)), ((), ())), preferred_element_type=jnp.float32
    )


def contract_first(left_rows, right_rows):
    return lax.dot_general(
        left_rows, right_rows, (((0,), (0,)), ((), ())), preferred_element_type=jnp.float32
    )


def block_pass(rows_in, rows_cot, norm_gain, gate_block, up_block, down_block):
    wide_in = rows_in.astype(jnp.float32)
    inv_rms = lax.rsqrt(jnp.mean(wide_in * wide_in, axis=-1, keepdims=True) + norm_eps)
    normed = (wide_in * inv_rms * norm_gain).astype(jnp.bfloat16)
    gate_pre = jnp.dot(normed, gate_block, preferred_element_type=jnp.float32)
    up_pre = jnp.dot(normed, up_block, preferred_element_type=jnp.float32)
    sigmoid_gate = jax.nn.sigmoid(gate_pre)
    activated = gate_pre * sigmoid_gate
    hidden = (activated * up_pre).astype(jnp.bfloat16)
    layer_rows = (wide_in + contract_last(hidden, down_block)).astype(jnp.bfloat16)
    d_hidden = jnp.dot(rows_cot, down_block, preferred_element_type=jnp.float32)
    d_gate = (d_hidden * up_pre * sigmoid_gate * (1.0 + gate_pre * (1.0 - sigmoid_gate))).astype(
        jnp.bfloat16
    )
    d_up = (d_hidden * activated).astype(jnp.bfloat16)
    d_normed = contract_last(d_gate, gate_block) + contract_last(d_up, up_block)
    scaled_grad = d_normed * norm_gain
    along = jnp.mean(scaled_grad * wide_in, axis=-1, keepdims=True)
    grad_rows = (
        rows_cot.astype(jnp.float32) + inv_rms * (scaled_grad - wide_in * inv_rms * inv_rms * along)
    ).astype(jnp.bfloat16)
    partials = (
        contract_first(normed, d_gate),
        contract_first(normed, d_up),
        contract_first(rows_cot, hidden),
    )
    return (layer_rows, grad_rows, partials)


def local(inputs, upstream, norm_gain, gate_weight, up_weight, down_weight):
    moved_gate, moved_up, moved_down = shifted((gate_weight, up_weight, down_weight), "blk", 1)
    gate_block, up_block, down_block = (
        lax.all_gather(moved_gate, "dp", axis=0, tiled=True),
        lax.all_gather(moved_up, "dp", axis=0, tiled=True),
        lax.all_gather(moved_down, "dp", axis=0, tiled=True),
    )
    layer_out, grad_input, partials = block_pass(
        inputs, upstream, norm_gain, gate_block, up_block, down_block
    )
    back_gate, back_up, back_down = shifted(
        (
            partials[0].astype(jnp.bfloat16),
            partials[1].astype(jnp.bfloat16),
            partials[2].astype(jnp.bfloat16),
        ),
        "blk",
        -1,
    )
    sum_gate, sum_up, sum_down = (
        lax.psum_scatter(
            back_gate.astype(jnp.float32).astype(jnp.bfloat16),
            "dp",
            scatter_dimension=0,
            tiled=True,
        ).astype(jnp.float32),
        lax.psum_scatter(
            back_up.astype(jnp.float32).astype(jnp.bfloat16), "dp", scatter_dimension=0, tiled=True
        ).astype(jnp.float32),
        lax.psum_scatter(
            back_down.astype(jnp.float32).astype(jnp.bfloat16),
            "dp",
            scatter_dimension=0,
            tiled=True,
        ).astype(jnp.float32),
    )
    grad_gate = sum_gate.astype(jnp.bfloat16)
    grad_up = sum_up.astype(jnp.bfloat16)
    grad_down = sum_down.astype(jnp.bfloat16)
    return (layer_out, grad_input, grad_gate, grad_up, grad_down)


def solution(mesh):
    placed = (
        P(("blk", "dp"), None),
        P(("blk", "dp"), None),
        P(),
        P("dp", "blk"),
        P("dp", "blk"),
        P("dp", "blk"),
    )
    return jax.shard_map(
        local,
        mesh=mesh,
        in_specs=placed,
        out_specs=(
            P(("blk", "dp"), None),
            P(("blk", "dp"), None),
            P("dp", "blk"),
            P("dp", "blk"),
            P("dp", "blk"),
        ),
        check_vma=False,
    )
```

profile of v0, /device:TPU:1, one launch (start us, length us, event | category | flops | bytes accessed | tf_op | source)
XLA Modules:
  0.0 635.4 jit_solution(10754833733964159748)
XLA Ops:
  9.9 7.0 %collective-permute-done.2 = bf16[640,448]{0,1:T(8,128)(2,1)S(1)} collective-permute-done((bf16[640,448]{0,1:T(8,128)(2,1)}, bf16[640,448]{0,1:T(8,128)(2,1)S(1)}, u32[]{:S(2)}, u32[]{:S(2)}) %collective-permute-start.2) | collective-permute-done | bytes 573472 | tf_op jit(solution)/shard_map/ppermute | solution.py:11
  20.2 7.0 %collective-permute-done.1 = bf16[640,448]{0,1:T(8,128)(2,1)S(1)} collective-permute-done((bf16[640,448]{0,1:T(8,128)(2,1)}, bf16[640,448]{0,1:T(8,128)(2,1)S(1)}, u32[]{:S(2)}, u32[]{:S(2)}) %collective-permute-start.1) | collective-permute-done | bytes 573472 | tf_op jit(solution)/shard_map/ppermute | solution.py:11
  30.5 13.1 %collective-permute-done = bf16[640,448]{0,1:T(8,128)(2,1)S(1)} collective-permute-done((bf16[640,448]{0,1:T(8,128)(2,1)}, bf16[640,448]{0,1:T(8,128)(2,1)S(1)}, u32[]{:S(2)}, u32[]{:S(2)}) %collective-permute-start) | collective-permute-done | bytes 573472 | tf_op jit(solution)/shard_map/ppermute | solution.py:11
  44.5 3.0 fusion.8
  47.5 50.9 %all-gather.8.cloned.1.call-done = bf16[5120,448]{0,1:T(8,128)(2,1)} async-done(((bf16[640,448]{0,1:T(8,128)(2,1)}), bf16[5120,448]{0,1:T(8,128)(2,1)}) %all-gather.8.cloned.1.call-update) | async-done | bytes 4587536 | tf_op jit(solution)/shard_map/all_gather | solution.py:60
  98.4 6.0 fusion.19
  104.4 69.2 %all-gather.6.cloned.1.call-done = bf16[5120,448]{0,1:T(8,128)(2,1)} async-done(((bf16[640,448]{0,1:T(8,128)(2,1)}), bf16[5120,448]{0,1:T(8,128)(2,1)}) %all-gather.6.cloned.1.call-update) | async-done | bytes 4587536 | tf_op jit(solution)/shard_map/all_gather | solution.py:59
  173.6 6.1 fusion.15
  179.7 69.2 %all-gather.4.cloned.1.call-done = bf16[5120,448]{0,1:T(8,128)(2,1)} async-done(((bf16[640,448]{0,1:T(8,128)(2,1)}), bf16[5120,448]{0,1:T(8,128)(2,1)}) %all-gather.4.cloned.1.call-update) | async-done | bytes 4587536 | tf_op jit(solution)/shard_map/all_gather | solution.py:58
  248.9 6.5 %multiply_convert_fusion.1 = (bf16[384,448]{0,1:T(8,128)(2,1)S(1)}, bf16[384,448]{0,1:T(8,128)(2,1)S(1)}, bf16[384,448]{0,1:T(8,128)(2,1)S(1)}) fusion(f32[384,448]{0,1:T(8,128)S(1)} %fusion.19, f32[384,448]{0,1:T(8,128)S(1)} %fusion.15, bf16[5120,448]{0,1:T(8,128)(2,1)} %all-gather.4.cloned.1.call-done, bf16[384,5120]{1,0:T(8,128)(2,1)} %param.6, ...), kind=kOutput, calls=%fused_computation.21 | convolution fusion | flops 1772052480 | bytes 10950144 | tf_op jit(solution)/shard_map/dot_general | solution.py:30
  259.3 51.2 %collective-permute-done.3 = bf16[5120,448]{0,1:T(8,128)(2,1)} collective-permute-done((bf16[5120,448]{0,1:T(8,128)(2,1)S(1)}, bf16[5120,448]{0,1:T(8,128)(2,1)}, u32[]{:S(2)}, u32[]{:S(2)}) %collective-permute-start.3) | collective-permute-done | bytes 4587552 | tf_op jit(solution)/shard_map/ppermute | solution.py:11
  310.5 7.6 %copy.11 = bf16[5120,448]{1,0:T(8,128)(2,1)} copy(bf16[5120,448]{0,1:T(8,128)(2,1)} %collective-permute-done.3) | data formatting | bytes 9175040
  318.4 4.8 convolution_convert_fusion
  324.3 79.3 %collective-permute-done.4 = bf16[5120,448]{0,1:T(8,128)(2,1)} collective-permute-done((bf16[5120,448]{0,1:T(8,128)(2,1)S(1)}, bf16[5120,448]{0,1:T(8,128)(2,1)}, u32[]{:S(2)}, u32[]{:S(2)}) %collective-permute-start.4) | collective-permute-done | bytes 4587552 | tf_op jit(solution)/shard_map/ppermute | solution.py:11
  403.6 7.7 %copy.13 = bf16[5120,448]{1,0:T(8,128)(2,1)} copy(bf16[5120,448]{0,1:T(8,128)(2,1)} %collective-permute-done.4) | data formatting | bytes 9175040
  411.3 4.7 fusion.11
  416.7 73.0 %collective-permute-done.5 = bf16[5120,448]{0,1:T(8,128)(2,1)} collective-permute-done((bf16[5120,448]{0,1:T(8,128)(2,1)S(1)}, bf16[5120,448]{0,1:T(8,128)(2,1)}, u32[]{:S(2)}, u32[]{:S(2)}) %collective-permute-start.5) | collective-permute-done | bytes 4587552 | tf_op jit(solution)/shard_map/ppermute | solution.py:11
  489.7 7.7 %copy.15 = bf16[5120,448]{1,0:T(8,128)(2,1)} copy(bf16[5120,448]{0,1:T(8,128)(2,1)} %collective-permute-done.5) | data formatting | bytes 9175040
  497.4 4.8 fusion.20
  502.2 6.0 fusion.10
  508.2 4.3 fusion.9
  512.6 4.3 fusion.7
  519.0 13.8 %reduce-scatter.12.cloned.1.call-done = bf16[640,448]{1,0:T(8,128)(2,1)} async-done(((bf16[5120,448]{1,0:T(8,128)(2,1)}), bf16[640,448]{1,0:T(8,128)(2,1)}) %reduce-scatter.12.cloned.1.call-update) | async-done | bytes 573456
  535.0 91.4 %reduce-scatter.14.cloned.1.call-done = bf16[640,448]{1,0:T(8,128)(2,1)} async-done(((bf16[5120,448]{1,0:T(8,128)(2,1)}), bf16[640,448]{1,0:T(8,128)(2,1)}) %reduce-scatter.14.cloned.1.call-update) | async-done | bytes 573456
  (44 shorter events, 22.7 us)
Async XLA Ops:
  7.2 91.2 %all-gather.8.cloned.1.call-start = ((), (), s32[]{:S(2)}) async-start(), calls=%async_computation.5 | async-start | bytes 5160960 | tf_op jit(solution)/shard_map/all_gather | solution.py:60
  7.2 9.6 %collective-permute-start.2 = (bf16[640,448]{0,1:T(8,128)(2,1)}, bf16[640,448]{0,1:T(8,128)(2,1)S(1)}, u32[]{:S(2)}, u32[]{:S(2)}) collective-permute-start(bf16[640,448]{0,1:T(8,128)(2,1)} %param.11), channel_id=1, source_target_pairs={{0,8},{8,16},{16,24},{24,32},{32,40},{40,48},{48,56},{56,64},{64,7... | collective-permute-start | bytes 1720328 | tf_op jit(solution)/shard_map/ppermute | solution.py:11
  16.9 0.8 copy-start.3
  17.7 155.9 %all-gather.6.cloned.1.call-start = ((), (), s32[]{:S(2)}) async-start(), calls=%async_computation.4 | async-start | bytes 5160960 | tf_op jit(solution)/shard_map/all_gather | solution.py:59
  17.7 9.4 %collective-permute-start.1 = (bf16[640,448]{0,1:T(8,128)(2,1)}, bf16[640,448]{0,1:T(8,128)(2,1)S(1)}, u32[]{:S(2)}, u32[]{:S(2)}) collective-permute-start(bf16[640,448]{0,1:T(8,128)(2,1)} %param.10), channel_id=1, source_target_pairs={{0,8},{8,16},{16,24},{24,32},{32,40},{40,48},{48,56},{56,64},{64,7... | collective-permute-start | bytes 1720328 | tf_op jit(solution)/shard_map/ppermute | solution.py:11
  27.1 0.8 copy-start.4
  28.0 220.9 %all-gather.4.cloned.1.call-start = ((), (), s32[]{:S(2)}) async-start(), calls=%async_computation.3 | async-start | bytes 5160960 | tf_op jit(solution)/shard_map/all_gather | solution.py:58
  28.0 15.6 %collective-permute-start = (bf16[640,448]{0,1:T(8,128)(2,1)}, bf16[640,448]{0,1:T(8,128)(2,1)S(1)}, u32[]{:S(2)}, u32[]{:S(2)}) collective-permute-start(bf16[640,448]{0,1:T(8,128)(2,1)} %param.9), channel_id=1, source_target_pairs={{0,8},{8,16},{16,24},{24,32},{32,40},{40,48},{48,56},{56,64},{64,7... | collective-permute-start | bytes 1720328 | tf_op jit(solution)/shard_map/ppermute | solution.py:11
  43.6 0.8 copy-start.5
  44.4 472.5 %reduce-scatter.10.cloned.1.call-start = ((), (), s32[]{:S(2)}) async-start(), calls=%async_computation.6 | async-start | bytes 5898240
  47.4 126.2 %copy-start.6 = (f32[5120]{0:T(1024)S(1)}, f32[5120]{0:T(1024)}, u32[]{:S(2)}) copy-start(f32[5120]{0:T(1024)} %param.8) | copy-start | bytes 61444
  248.9 6.5 %copy-start = (bf16[384,5120]{1,0:T(8,128)(2,1)S(1)}, bf16[384,5120]{1,0:T(8,128)(2,1)}, u32[]{:S(2)}) copy-start(bf16[384,5120]{1,0:T(8,128)(2,1)} %param.6) | copy-start | bytes 11796484
  258.2 52.3 %collective-permute-start.3 = (bf16[5120,448]{0,1:T(8,128)(2,1)S(1)}, bf16[5120,448]{0,1:T(8,128)(2,1)}, u32[]{:S(2)}, u32[]{:S(2)}) collective-permute-start(bf16[5120,448]{0,1:T(8,128)(2,1)S(1)} %convolution_convert_fusion.1), channel_id=1, source_target_pairs={{0,120},{8,0},{16,8},{24,16},{32,24},{40,32},{48,40},{56,48},{64,5... | collective-permute-start | bytes 13762568 | tf_op jit(solution)/shard_map/ppermute | solution.py:11
  318.1 214.7 %reduce-scatter.12.cloned.1.call-start = ((), (), s32[]{:S(2)}) async-start(), calls=%async_computation.7 | async-start | bytes 5898240
  323.1 80.4 %collective-permute-start.4 = (bf16[5120,448]{0,1:T(8,128)(2,1)S(1)}, bf16[5120,448]{0,1:T(8,128)(2,1)}, u32[]{:S(2)}, u32[]{:S(2)}) collective-permute-start(bf16[5120,448]{0,1:T(8,128)(2,1)S(1)} %convolution_convert_fusion), channel_id=1, source_target_pairs={{0,120},{8,0},{16,8},{24,16},{32,24},{40,32},{48,40},{56,48},{64,5... | collective-permute-start | bytes 13762568 | tf_op jit(solution)/shard_map/ppermute | solution.py:11
  411.3 215.2 %reduce-scatter.14.cloned.1.call-start = ((), (), s32[]{:S(2)}) async-start(), calls=%async_computation.8 | async-start | bytes 5898240
  416.0 73.7 %collective-permute-start.5 = (bf16[5120,448]{0,1:T(8,128)(2,1)S(1)}, bf16[5120,448]{0,1:T(8,128)(2,1)}, u32[]{:S(2)}, u32[]{:S(2)}) collective-permute-start(bf16[5120,448]{0,1:T(8,128)(2,1)S(1)} %fusion.11), channel_id=1, source_target_pairs={{0,120},{8,0},{16,8},{24,16},{32,24},{40,32},{48,40},{56,48},{64,5... | collective-permute-start | bytes 13762568 | tf_op jit(solution)/shard_map/ppermute | solution.py:11
  497.4 4.8 copy-start.1
  497.4 10.8 %slice-start = ((s8[4587520]{0:T(1024)(128)(4,1)}), s8[4194304]{0:T(1024)(128)(4,1)S(1)}, s32[]{:S(2)}) async-start(s8[4587520]{0:T(1024)(128)(4,1)} %bitcast.19), calls=%async_computation.9 | async-start | bytes 8388608
  502.2 6.0 slice-start.1
  508.2 4.4 copy-start.2
Sparse Core Ops, SparseCore 0:
  17.8 80.5 all-gather.7
  101.3 72.2 all-gather.5
  176.6 72.2 all-gather.3
  318.2 107.8 reduce-scatter.9
  429.9 102.9 reduce-scatter.11
  536.6 89.8 reduce-scatter.13
where the time goes:
time: 636 us; the launch traced here: 635 us
  waiting for transfers between devices  525 us (83%)
  matrix products  46 us (7%)
  local copies, waits for them, and re-layouts  31.9 us (5%)
  between operations  14.2 us (2%)
  starting transfers between devices  10.9 us (2%)
  other arithmetic  7.29 us (1%)
    ppermute x6, waiting for transfers between devices, shifted(): lax.ppermute(value, axis, [(i, (i + by) % size) for i in range(size)])  230 us
    unnamed x9, waiting for transfers between devices  105 us
    all_gather x1, waiting for transfers between devices, local(): lax.all_gather(moved_up, 'dp', axis=0, tiled=True)  69.2 us
    all_gather x1, waiting for transfers between devices, local(): lax.all_gather(moved_gate, 'dp', axis=0, tiled=True)  69.2 us
    all_gather x1, waiting for transfers between devices, local(): lax.all_gather(moved_down, 'dp', axis=0, tiled=True)  50.9 us
    unnamed x24, local copies, waits for them, and re-layouts  31.9 us
    dot_general x3, matrix products, contract_last(): lax.dot_general(left_rows, right_rows, (((1,), (1,)), ((), ())), preferre...  15.1 us
  transfers between devices with their start and end apart: 12, of which 11 were waited for; matrix products, arithmetic and copies ran while one was open for 10% of the time, Pallas kernels for 0%

commit v1 on v0

--- a/solution.py
+++ b/solution.py
@@ -62,35 +62,11 @@
     layer_out, grad_input, partials = block_pass(
         inputs, upstream, norm_gain, gate_block, up_block, down_block
     )
-    back_gate, back_up, back_down = shifted(
-        (
-            partials[0].astype(jnp.bfloat16),
-            partials[1].astype(jnp.bfloat16),
-            partials[2].astype(jnp.bfloat16),
-        ),
-        "blk",
-        -1,
+    sums = tuple(
+        lax.psum_scatter(p.astype(jnp.bfloat16), "dp", scatter_dimension=0, tiled=True)
+        for p in partials
     )
-    sum_gate, sum_up, sum_down = (
-        lax.psum_scatter(
-            back_gate.astype(jnp.float32).astype(jnp.bfloat16),
-            "dp",
-            scatter_dimension=0,
-            tiled=True,
-        ).astype(jnp.float32),
-        lax.psum_scatter(
-            back_up.astype(jnp.float32).astype(jnp.bfloat16), "dp", scatter_dimension=0, tiled=True
-        ).astype(jnp.float32),
-        lax.psum_scatter(
-            back_down.astype(jnp.float32).astype(jnp.bfloat16),
-            "dp",
-            scatter_dimension=0,
-            tiled=True,
-        ).astype(jnp.float32),
-    )
-    grad_gate = sum_gate.astype(jnp.bfloat16)
-    grad_up = sum_up.astype(jnp.bfloat16)
-    grad_down = sum_down.astype(jnp.bfloat16)
+    grad_gate, grad_up, grad_down = shifted(sums, "blk", -1)
     return (layer_out, grad_input, grad_gate, grad_up, grad_down)
 
 

time: 636 us -> 564 us (0.89)
  waiting for transfers between devices: 525 us -> 442 us
  matrix products: 46 us -> 53.3 us
    ppermute x6, waiting for transfers between devices: 230 us -> 27.2 us  [shifted(): lax.ppermute(value, axis, [(i, (i + by) % size) for i in range(size)])]
    unnamed x9, waiting for transfers between devices: 105 us -> 226 us
    dot_general x3, matrix products: 12.2 us -> 18.6 us  [contract_first(): lax.dot_general(left_rows, right_rows, (((0,), (0,)), ((), ())), preferre...]
    unnamed x24 -> x25, local copies, waits for them, and re-layouts: 31.9 us -> 32.4 us
  transfers between devices with their start and end apart: 12 -> 12, of which waited for: 11 -> 10; matrix products, arithmetic and copies ran while one was open for 10% -> 13% of each run, Pallas kernels for 0% -> 0%
where the time goes in v1:
time: 564 us; the launch traced here: 563 us
  waiting for transfers between devices  442 us (78%)
  matrix products  53.3 us (9%)
  local copies, waits for them, and re-layouts  32.4 us (6%)
  between operations  14.2 us (3%)
  starting transfers between devices  12.3 us (2%)
  other arithmetic  8.88 us (2%)
    unnamed x9, waiting for transfers between devices  226 us
    all_gather x1, waiting for transfers between devices, local(): lax.all_gather(moved_up, 'dp', axis=0, tiled=True)  69.2 us
    all_gather x1, waiting for transfers between devices, local(): lax.all_gather(moved_gate, 'dp', axis=0, tiled=True)  69.2 us
    all_gather x1, waiting for transfers between devices, local(): lax.all_gather(moved_down, 'dp', axis=0, tiled=True)  50.9 us
    unnamed x25, local copies, waits for them, and re-layouts  32.4 us
    ppermute x6, waiting for transfers between devices, shifted(): lax.ppermute(value, axis, [(i, (i + by) % size) for i in range(size)])  27.2 us
    dot_general x3, matrix products, contract_first(): lax.dot_general(left_rows, right_rows, (((0,), (0,)), ((), ())), preferre...  18.6 us
    dot_general x3, matrix products, contract_last(): lax.dot_general(left_rows, right_rows, (((1,), (1,)), ((), ())), preferre...  16 us
  transfers between devices with their start and end apart: 12, of which 10 were waited for; matrix products, arithmetic and copies ran while one was open for 13% of the time, Pallas kernels for 0%

profile of v1, /device:TPU:1, one launch (start us, length us, event | category | flops | bytes accessed | tf_op | source)
XLA Modules:
  0.0 563.2 jit_solution(15751496102506818388)
XLA Ops:
  7.2 2.7 collective-permute-start.2
  9.9 7.0 %collective-permute-done.2 = bf16[640,448]{0,1:T(8,128)(2,1)S(1)} collective-permute-done((bf16[640,448]{0,1:T(8,128)(2,1)}, bf16[640,448]{0,1:T(8,128)(2,1)S(1)}, u32[]{:S(2)}, u32[]{:S(2)}) %collective-permute-start.2) | collective-permute-done | bytes 573472 | tf_op jit(solution)/shard_map/ppermute | solution.py:11
  20.2 7.0 %collective-permute-done.1 = bf16[640,448]{0,1:T(8,128)(2,1)S(1)} collective-permute-done((bf16[640,448]{0,1:T(8,128)(2,1)}, bf16[640,448]{0,1:T(8,128)(2,1)S(1)}, u32[]{:S(2)}, u32[]{:S(2)}) %collective-permute-start.1) | collective-permute-done | bytes 573472 | tf_op jit(solution)/shard_map/ppermute | solution.py:11
  30.5 13.1 %collective-permute-done = bf16[640,448]{0,1:T(8,128)(2,1)S(1)} collective-permute-done((bf16[640,448]{0,1:T(8,128)(2,1)}, bf16[640,448]{0,1:T(8,128)(2,1)S(1)}, u32[]{:S(2)}, u32[]{:S(2)}) %collective-permute-start) | collective-permute-done | bytes 573472 | tf_op jit(solution)/shard_map/ppermute | solution.py:11
  44.5 3.0 fusion.8
  47.5 50.9 %all-gather.8.cloned.1.call-done = bf16[5120,448]{0,1:T(8,128)(2,1)} async-done(((bf16[640,448]{0,1:T(8,128)(2,1)}), bf16[5120,448]{0,1:T(8,128)(2,1)}) %all-gather.8.cloned.1.call-update) | async-done | bytes 4587536 | tf_op jit(solution)/shard_map/all_gather | solution.py:60
  98.4 6.0 %fusion.19 = f32[384,448]{0,1:T(8,128)S(1)} fusion(bf16[384,5120]{1,0:T(8,128)(2,1)} %param.7, bf16[5120,448]{0,1:T(8,128)(2,1)} %all-gather.8.cloned.1.call-done), kind=kOutput, calls=%fused_computation.29 | convolution fusion | flops 1761607680 | bytes 9207808 | tf_op jit(solution)/shard_map/dot_general | solution.py:36
  104.4 69.2 %all-gather.6.cloned.1.call-done = bf16[5120,448]{0,1:T(8,128)(2,1)} async-done(((bf16[640,448]{0,1:T(8,128)(2,1)}), bf16[5120,448]{0,1:T(8,128)(2,1)}) %all-gather.6.cloned.1.call-update) | async-done | bytes 4587536 | tf_op jit(solution)/shard_map/all_gather | solution.py:59
  173.6 6.1 %fusion.15 = f32[384,448]{0,1:T(8,128)S(1)} fusion(bf16[5120,448]{0,1:T(8,128)(2,1)} %all-gather.6.cloned.1.call-done, bf16[384,5120]{1,0:T(8,128)(2,1)} %param.6, f32[5120]{0:T(1024)S(1)} %copy-done.5, f32[384]{0:T(512)S(1)} %add_rsqrt_fusion), kind=kOutput, calls=%fused_computation.27 | convolution fusion | flops 1769472000 | bytes 9229824 | tf_op jit(solution)/shard_map/dot_general | solution.py:31
  179.7 69.2 %all-gather.4.cloned.1.call-done = bf16[5120,448]{0,1:T(8,128)(2,1)} async-done(((bf16[640,448]{0,1:T(8,128)(2,1)}), bf16[5120,448]{0,1:T(8,128)(2,1)}) %all-gather.4.cloned.1.call-update) | async-done | bytes 4587536 | tf_op jit(solution)/shard_map/all_gather | solution.py:58
  248.9 6.5 %multiply_convert_fusion.1 = (bf16[384,448]{0,1:T(8,128)(2,1)S(1)}, bf16[384,448]{0,1:T(8,128)(2,1)S(1)}, bf16[384,448]{0,1:T(8,128)(2,1)S(1)}) fusion(f32[384,448]{0,1:T(8,128)S(1)} %fusion.19, f32[384,448]{0,1:T(8,128)S(1)} %fusion.15, bf16[5120,448]{0,1:T(8,128)(2,1)} %all-gather.4.cloned.1.call-done, bf16[384,5120]{1,0:T(8,128)(2,1)} %param.6, ...), kind=kOutput, calls=%fused_computation.21 | convolution fusion | flops 1772052480 | bytes 10950144 | tf_op jit(solution)/shard_map/dot_general | solution.py:30
  255.4 4.7 fusion.11
  260.1 7.7 %copy.15 = bf16[5120,448]{1,0:T(8,128)(2,1)} copy(bf16[5120,448]{0,1:T(8,128)(2,1)} %fusion.11) | data formatting | bytes 9175040
  268.1 7.0 %convolution_convert_fusion.1 = bf16[5120,448]{0,1:T(8,128)(2,1)} fusion(bf16[384,448]{0,1:T(8,128)(2,1)S(1)} %get-tuple-element.5, bf16[384,5120]{1,0:T(8,128)(2,1)} %param.6, f32[5120]{0:T(1024)S(1)} %copy-done.5, f32[384]{0:T(512)S(1)} %add_rsqrt_fusion), kind=kOutput, calls=%fused_computation.17 | convolution fusion | flops 1771765760 | bytes 8885760 | tf_op jit(solution)/shard_map/dot_general | solution.py:21
  275.0 7.9 %copy.11 = bf16[5120,448]{1,0:T(8,128)(2,1)} copy(bf16[5120,448]{0,1:T(8,128)(2,1)} %convolution_convert_fusion.1) | data formatting | bytes 9175040
  283.0 6.9 %convolution_convert_fusion = bf16[5120,448]{0,1:T(8,128)(2,1)} fusion(bf16[384,448]{0,1:T(8,128)(2,1)S(1)} %get-tuple-element.6, bf16[384,5120]{1,0:T(8,128)(2,1)} %param.6, f32[5120]{0:T(1024)S(1)} %copy-done.5, f32[384]{0:T(512)S(1)} %add_rsqrt_fusion), kind=kOutput, calls=%fused_computation.16 | convolution fusion | flops 1771765760 | bytes 8885760 | tf_op jit(solution)/shard_map/dot_general | solution.py:21
  289.9 7.7 %copy.13 = bf16[5120,448]{1,0:T(8,128)(2,1)} copy(bf16[5120,448]{0,1:T(8,128)(2,1)} %convolution_convert_fusion) | data formatting | bytes 9175040
  297.6 4.8 fusion.20
  302.6 3.6 fusion.10
  306.2 5.9 %fusion.7 = bf16[384,5120]{1,0:T(8,128)(2,1)} fusion(f32[384,5120]{1,0:T(8,128)S(1)} %get-tuple-element.9, bf16[384,5120]{1,0:T(8,128)(2,1)S(1)} %copy-done, bf16[384,5120]{1,0:T(8,128)(2,1)} %param.7, f32[384]{0:T(512)S(1)} %broadcast_multiply_fusion, f32[384]{0:T(512)S(1)} %add_rsqrt_fusion), kind=kLoop, calls=%fused_computation.11 | loop fusion | flops 17694720 | bytes 19663872 | tf_op jit(solution)/shard_map/convert_element_type | solution.py:46
  312.1 44.2 %reduce-scatter.14.cloned.1.call-done = bf16[640,448]{1,0:T(8,128)(2,1)} async-done(((bf16[5120,448]{1,0:T(8,128)(2,1)}), bf16[640,448]{1,0:T(8,128)(2,1)}) %reduce-scatter.14.cloned.1.call-update) | async-done | bytes 573456
  359.3 90.5 %reduce-scatter.10.cloned.1.call-done = bf16[640,448]{1,0:T(8,128)(2,1)} async-done(((bf16[5120,448]{1,0:T(8,128)(2,1)}), bf16[640,448]{1,0:T(8,128)(2,1)}) %reduce-scatter.10.cloned.1.call-update) | async-done | bytes 573456
  452.6 90.8 %reduce-scatter.12.cloned.1.call-done = bf16[640,448]{1,0:T(8,128)(2,1)} async-done(((bf16[5120,448]{1,0:T(8,128)(2,1)}), bf16[640,448]{1,0:T(8,128)(2,1)}) %reduce-scatter.12.cloned.1.call-update) | async-done | bytes 573456
  546.0 7.7 %fusion.9 = bf16[384,5120]{1,0:T(8,128)(2,1)} fusion(bf16[384,5120]{1,0:T(8,128)(2,1)} %param.6, bf16[384,448]{0,1:T(8,128)(2,1)S(1)} %get-tuple-element.7, bf16[5120,448]{0,1:T(8,128)(2,1)} %all-gather.8.cloned.1.call-done), kind=kOutput, calls=%fused_computation.13 | convolution fusion | flops 1767505920 | bytes 12795904 | tf_op jit(solution)/shard_map/dot_general | solution.py:15
  (45 shorter events, 19.1 us)
Async XLA Ops:
  7.2 91.2 %all-gather.8.cloned.1.call-start = ((), (), s32[]{:S(2)}) async-start(), calls=%async_computation.5 | async-start | bytes 5160960 | tf_op jit(solution)/shard_map/all_gather | solution.py:60
  7.2 9.6 %collective-permute-start.2 = (bf16[640,448]{0,1:T(8,128)(2,1)}, bf16[640,448]{0,1:T(8,128)(2,1)S(1)}, u32[]{:S(2)}, u32[]{:S(2)}) collective-permute-start(bf16[640,448]{0,1:T(8,128)(2,1)} %param.11), channel_id=1, source_target_pairs={{0,8},{8,16},{16,24},{24,32},{32,40},{40,48},{48,56},{56,64},{64,7... | collective-permute-start | bytes 1720328 | tf_op jit(solution)/shard_map/ppermute | solution.py:11
  16.9 0.8 copy-start.2
  17.7 155.9 %all-gather.6.cloned.1.call-start = ((), (), s32[]{:S(2)}) async-start(), calls=%async_computation.4 | async-start | bytes 5160960 | tf_op jit(solution)/shard_map/all_gather | solution.py:59
  17.7 9.4 %collective-permute-start.1 = (bf16[640,448]{0,1:T(8,128)(2,1)}, bf16[640,448]{0,1:T(8,128)(2,1)S(1)}, u32[]{:S(2)}, u32[]{:S(2)}) collective-permute-start(bf16[640,448]{0,1:T(8,128)(2,1)} %param.10), channel_id=1, source_target_pairs={{0,8},{8,16},{16,24},{24,32},{32,40},{40,48},{48,56},{56,64},{64,7... | collective-permute-start | bytes 1720328 | tf_op jit(solution)/shard_map/ppermute | solution.py:11
  27.1 0.8 copy-start.3
  28.0 220.9 %all-gather.4.cloned.1.call-start = ((), (), s32[]{:S(2)}) async-start(), calls=%async_computation.3 | async-start | bytes 5160960 | tf_op jit(solution)/shard_map/all_gather | solution.py:58
  28.0 15.6 %collective-permute-start = (bf16[640,448]{0,1:T(8,128)(2,1)}, bf16[640,448]{0,1:T(8,128)(2,1)S(1)}, u32[]{:S(2)}, u32[]{:S(2)}) collective-permute-start(bf16[640,448]{0,1:T(8,128)(2,1)} %param.9), channel_id=1, source_target_pairs={{0,8},{8,16},{16,24},{24,32},{32,40},{40,48},{48,56},{56,64},{64,7... | collective-permute-start | bytes 1720328 | tf_op jit(solution)/shard_map/ppermute | solution.py:11
  43.6 0.8 copy-start.4
  44.4 311.9 %reduce-scatter.14.cloned.1.call-start = ((), (), s32[]{:S(2)}) async-start(), calls=%async_computation.8 | async-start | bytes 5898240
  47.4 126.2 %copy-start.5 = (f32[5120]{0:T(1024)S(1)}, f32[5120]{0:T(1024)}, u32[]{:S(2)}) copy-start(f32[5120]{0:T(1024)} %param.8) | copy-start | bytes 61444
  248.9 6.5 %copy-start.1 = (bf16[384,5120]{1,0:T(8,128)(2,1)S(1)}, bf16[384,5120]{1,0:T(8,128)(2,1)}, u32[]{:S(2)}) copy-start(bf16[384,5120]{1,0:T(8,128)(2,1)} %param.7) | copy-start | bytes 11796484
  267.8 182.0 %reduce-scatter.10.cloned.1.call-start = ((), (), s32[]{:S(2)}) async-start(), calls=%async_computation.6 | async-start | bytes 5898240
  282.9 260.4 %reduce-scatter.12.cloned.1.call-start = ((), (), s32[]{:S(2)}) async-start(), calls=%async_computation.7 | async-start | bytes 5898240
  297.6 4.9 slice-start
  297.6 4.8 copy-start
  297.6 5.0 slice-start.1
  357.7 196.1 %collective-permute-start.5 = (bf16[640,448]{0,1:T(8,128)(2,1)S(1)}, bf16[640,448]{0,1:T(8,128)(2,1)S(1)}, u32[]{:S(2)}, u32[]{:S(2)}) collective-permute-start(bf16[640,448]{0,1:T(8,128)(2,1)S(1)} %copy.16), channel_id=1, source_target_pairs={{0,120},{8,0},{16,8},{24,16},{32,24},{40,32},{48,40},{56,48},{64,5... | collective-permute-start | bytes 1720328 | tf_op jit(solution)/shard_map/ppermute | solution.py:11
  451.2 102.6 %collective-permute-start.3 = (bf16[640,448]{0,1:T(8,128)(2,1)S(1)}, bf16[640,448]{0,1:T(8,128)(2,1)S(1)}, u32[]{:S(2)}, u32[]{:S(2)}) collective-permute-start(bf16[640,448]{0,1:T(8,128)(2,1)S(1)} %copy.12), channel_id=1, source_target_pairs={{0,120},{8,0},{16,8},{24,16},{32,24},{40,32},{48,40},{56,48},{64,5... | collective-permute-start | bytes 1720328 | tf_op jit(solution)/shard_map/ppermute | solution.py:11
  544.7 9.2 %collective-permute-start.4 = (bf16[640,448]{0,1:T(8,128)(2,1)S(1)}, bf16[640,448]{0,1:T(8,128)(2,1)S(1)}, u32[]{:S(2)}, u32[]{:S(2)}) collective-permute-start(bf16[640,448]{0,1:T(8,128)(2,1)S(1)} %copy.14), channel_id=1, source_target_pairs={{0,120},{8,0},{16,8},{24,16},{32,24},{40,32},{48,40},{56,48},{64,5... | collective-permute-start | bytes 1720328 | tf_op jit(solution)/shard_map/ppermute | solution.py:11
Sparse Core Ops, SparseCore 0:
  17.8 80.5 all-gather.7
  101.3 72.2 all-gather.5
  176.6 72.2 all-gather.3
  268.0 88.2 reduce-scatter.13
  360.0 89.7 reduce-scatter.9
  453.5 89.7 reduce-scatter.11

commit v2 on v1

v2 whole, which is shorter than its diff:
```python
import functools

import jax
import jax.numpy as jnp
from jax import lax
from jax.experimental import pallas as pl
from jax.experimental.pallas import tpu as pltpu
from jax.sharding import PartitionSpec as P

norm_eps = 1e-05
MESH = pl.DeviceIdType.MESH
F32, BF16 = jnp.float32, jnp.bfloat16

CHUNK = {("a", 0): 0, ("b", 0): 1, ("a", 1): 2, ("b", 1): 3, ("a", 2): 4, ("b", 2): 5, ("a", 3): 6}
N_A, N_B, N_CHUNK = 4, 3, 7
SLOTS = 4
ORDER = (
    "a1.0 b1.0 b1.1 a1.1", "b1.2 a1.2 a2.0 b2.0", "b2.1 a1.3 a2.1 b2.2", "a2.2 a3.0 a2.3 b3.0",
    "a3.1 b3.1 a4.0 a4.1", "b3.2 b4.0 a5.0 a5.1", "b5.0 b4.1 b6.0 b5.1", "b6.1 b4.2 a3.2 b5.2",
    "a3.3 a6.0 a6.1 a4.2", "f.0 f.1 f.2 b6.2", "f.3 f.4 f.5 a4.3", "f.6 f.7 a5.2 a6.2",
    "a5.3 a6.3",
)


def nt(left, right):
    return lax.dot_general(left, right, (((1,), (1,)), ((), ())), preferred_element_type=F32)


def kernel(
    n_blk, x_any, up_any, gain_ref, own, lo_any, gi_any, g_ref,
    xin, up, normed, inv, wt, part, stage, rc1, rb1, ra1, ra2, rc2, rb2,
    hid_t, dg_t, du_t, hid, dg, du, along_t, along, ss, rs, ls,
):
    tok, width = xin.shape
    ff = wt.shape[1]
    ch = ff // N_CHUNK
    half = ch // 2
    sh = width // 8

    blk, dp = lax.axis_index("blk"), lax.axis_index("dp")
    xh, y = dp // 4, dp % 4
    nxt, prv = lax.rem(blk + 1, n_blk), lax.rem(blk + n_blk - 1, n_blk)
    yu, yd, yo = lax.rem(y + 1, 4), lax.rem(y + 3, 4), lax.rem(y + 2, 4)
    xo = 1 - xh
    up_dev, dn_dev = (blk, xh * 4 + yu), (blk, xh * 4 + yd)
    to_blk = ((nxt, dp), (nxt, xo * 4 + y))
    back_blk = ((prv, dp), (prv, xo * 4 + y))

    def lanes(owner, count=1):
        return pl.ds(pl.multiple_of(owner * sh, 128), count * sh)

    counter = [0]
    live = {}

    def send(name, src, dst, target):
        i = counter[0]
        counter[0] += 1
        cp = pltpu.make_async_remote_copy(
            src_ref=src, dst_ref=dst, send_sem=ss.at[i], recv_sem=rs.at[i],
            device_id=target, device_id_type=MESH,
        )
        cp.start()
        live.setdefault(name, []).append(cp)

    waited = set()

    def arrived(name):
        for cp in live[name]:
            cp.wait_recv()

    def sent(name):
        for cp in live[name]:
            cp.wait_send()
        waited.add(name)

    load_x = pltpu.make_async_copy(x_any, xin, ls.at[0])
    load_u = pltpu.make_async_copy(up_any, up, ls.at[1])
    load_x.start()
    load_u.start()

    barrier = pltpu.get_barrier_semaphore()
    for other in (up_dev, dn_dev) + to_blk + back_blk:
        pl.semaphore_signal(barrier, inc=1, device_id=other, device_id_type=MESH)
    pl.semaphore_wait(barrier, 6)

    def rows(c):
        return pl.ds(c * ch, ch)

    lo_half, hi_half = pl.ds(0, half), pl.ds(half, half)

    for j in range(max(N_A, N_B)):
        if j < N_A:
            c = CHUNK["a", j]
            for k in range(2):
                send(("A1", j), own.at[:, rows(c)], wt.at[:, rows(c), lanes(dp)], to_blk[k])
        if j < N_B:
            c = CHUNK["b", j]
            send(("B2", j), own.at[:, rows(c)], stage.at[j, 0], up_dev)
            send(("B2", j), own.at[:, rows(c)], stage.at[j, 1], dn_dev)
            for k in range(2):
                send(("A2", j), own.at[:, rows(c)], wt.at[:, rows(c), lanes(dp)], to_blk[k])

    load_x.wait()

    @pl.loop(0, tok // 16)
    def _(r):
        at = pl.ds(pl.multiple_of(r * 16, 16), 16)
        wide = xin[at, :].astype(F32)
        scale = lax.rsqrt(jnp.mean(wide * wide, axis=-1, keepdims=True) + norm_eps)
        inv[at, :] = jnp.broadcast_to(scale, (16, 128))
        normed[at, :] = (wide * scale * gain_ref[...]).astype(BF16)

    along_t[...] = jnp.zeros_like(along_t)
    load_u.wait()

    def compute(c):
        slot = c % SLOTS
        both = jnp.concatenate([wt[0, rows(c), :], wt[1, rows(c), :]], axis=0)
        pre = nt(both, normed[...])
        d_hidden = nt(wt[2, rows(c), :], up[...])
        gate, upp = pre[:ch], pre[ch:]
        sig = jax.nn.sigmoid(gate)
        act = gate * sig
        hidden = (act * upp).astype(BF16)
        d_gate = (d_hidden * upp * sig * (1.0 + gate * (1.0 - sig))).astype(BF16)
        d_up = (d_hidden * act).astype(BF16)
        hid_t[rows(c), :] = hidden
        dg_t[rows(c), :] = d_gate
        du_t[rows(c), :] = d_up
        summed = d_gate.astype(F32) * gate + d_up.astype(F32) * upp
        along_t[...] += jnp.broadcast_to(jnp.sum(summed, axis=0, keepdims=True), along_t.shape)

        @pl.loop(0, 8)
        def _(o):
            at = lanes(o)
            gu = jnp.concatenate([dg_t[rows(c), :], du_t[rows(c), :]], axis=0)
            pair = jnp.dot(gu, normed[:, at], preferred_element_type=F32)
            part[slot, 0, :, at] = pair[:ch].astype(BF16)
            part[slot, 1, :, at] = pair[ch:].astype(BF16)
            part[slot, 2, :, at] = jnp.dot(
                hid_t[rows(c), :], up[:, at], preferred_element_type=F32
            ).astype(BF16)

    def add(out, *terms):
        for w in range(3):
            total = terms[0][w].astype(F32)
            for term in terms[1:]:
                total = total + term[w].astype(F32)
            out[w] = total.astype(BF16)

    def reuse(c):
        if c >= SLOTS:
            old = {v: k for k, v in CHUNK.items()}[c - SLOTS]
            for name in ("c1", "b1", "a1") if old[0] == "a" else ("a2",):
                sent((name, old[1]))

    def a1(j, c):
        arrived(("A1", j))
        for x in range(2):
            at = lanes(4 * x + y)
            send(("B1", j), wt.at[:, rows(c), at], wt.at[:, rows(c), at], up_dev)
            send(("B1", j), wt.at[:, rows(c), at], wt.at[:, rows(c), at], dn_dev)

    def a2(j, c):
        arrived(("B1", j))
        low, high = pl.ds(c * ch, half), pl.ds(c * ch + half, half)
        for x in range(2):
            at = lanes(4 * x + yd)
            send(("C1", j), wt.at[:, low, at], wt.at[:, low, at], up_dev)
            at = lanes(4 * x + yu)
            send(("C1", j), wt.at[:, high, at], wt.at[:, high, at], dn_dev)

    def a3(j, c):
        arrived(("C1", j))
        reuse(c)
        compute(c)
        slot = c % SLOTS
        for x in range(2):
            at = lanes(4 * x + yo)
            send(("c1", j), part.at[slot, :, lo_half, at], rc1.at[j, 0, x], up_dev)
            send(("c1", j), part.at[slot, :, hi_half, at], rc1.at[j, 1, x], dn_dev)

    def a4(j, c):
        arrived(("c1", j))
        slot = c % SLOTS
        for x in range(2):
            at = lanes(4 * x + yu)
            mine = part.at[slot, :, lo_half, at]
            add(mine, mine, rc1.at[j, 0, x])
            send(("b1", j), part.at[slot, :, :, at], rb1.at[j, 0, x], up_dev)
            at = lanes(4 * x + yd)
            mine = part.at[slot, :, hi_half, at]
            add(mine, mine, rc1.at[j, 1, x])
            send(("b1", j), part.at[slot, :, :, at], rb1.at[j, 1, x], dn_dev)

    def a5(j, c):
        arrived(("b1", j))
        slot = c % SLOTS
        for x in range(2):
            mine = part.at[slot, :, :, lanes(4 * x + y)]
            add(mine, mine, rb1.at[j, 0, x], rb1.at[j, 1, x])
        for k in range(2):
            at = lanes(4 * (xh if k == 0 else xo) + y)
            send(("a1", j), part.at[slot, :, :, at], ra1.at[j, k], back_blk[k])

    def a6(j, c):
        arrived(("a1", j))
        add(g_ref.at[:, rows(c)], ra1.at[j, 0], ra1.at[j, 1])

    def b1(j, c):
        arrived(("B2", j))
        send(("C2", j), stage.at[j, 0, :, lo_half], stage.at[j, 2, :, lo_half], up_dev)
        send(("C2", j), stage.at[j, 1, :, hi_half], stage.at[j, 2, :, hi_half], dn_dev)
        for s, yy in ((0, yd), (1, yu)):
            for k in range(2):
                send(("A2", j), stage.at[j, s], wt.at[:, rows(c), lanes(xh * 4 + yy)], to_blk[k])

    def b2(j, c):
        arrived(("C2", j))
        for k in range(2):
            send(("A2", j), stage.at[j, 2], wt.at[:, rows(c), lanes(xh * 4 + yo)], to_blk[k])

    def b3(j, c):
        arrived(("A2", j))
        reuse(c)
        compute(c)
        slot = c % SLOTS
        for k in range(2):
            at = lanes(4 * (xh if k == 0 else xo), 4)
            send(("a2", j), part.at[slot, :, :, at], ra2.at[j, k], back_blk[k])

    def b4(j, c):
        arrived(("a2", j))
        add(ra2.at[j, 0], ra2.at[j, 0], ra2.at[j, 1])
        send(("c2", j), ra2.at[j, 0, :, lo_half, lanes(yo)], rc2.at[j, 0], up_dev)
        send(("c2", j), ra2.at[j, 0, :, hi_half, lanes(yo)], rc2.at[j, 1], dn_dev)

    def b5(j, c):
        arrived(("c2", j))
        mine = ra2.at[j, 0, :, lo_half, lanes(yu)]
        add(mine, mine, rc2.at[j, 0])
        send(("b2", j), ra2.at[j, 0, :, :, lanes(yu)], rb2.at[j, 0], up_dev)
        mine = ra2.at[j, 0, :, hi_half, lanes(yd)]
        add(mine, mine, rc2.at[j, 1])
        send(("b2", j), ra2.at[j, 0, :, :, lanes(yd)], rb2.at[j, 1], dn_dev)

    def b6(j, c):
        arrived(("b2", j))
        add(g_ref.at[:, rows(c)], ra2.at[j, 0, :, :, lanes(y)], rb2.at[j, 0], rb2.at[j, 1])

    stores = []

    def f(t):
        if t == 0:
            hid[...] = hid_t[...].T
            dg[...] = dg_t[...].T
            du[...] = du_t[...].T
            along[...] = along_t[...].T / (inv[...] * width)
        at = lanes(t)
        scale = inv[:, :1]
        wide = xin[:, at].astype(F32)
        out = jnp.dot(hid[...], wt[2, :, at], preferred_element_type=F32)
        normed[:, at] = (wide + out).astype(BF16)
        cp = pltpu.make_async_copy(normed.at[:, at], lo_any.at[:, at], ls.at[2 + 2 * t])
        cp.start()
        stores.append(cp)
        d_normed = jnp.dot(dg[...], wt[0, :, at], preferred_element_type=F32)
        d_normed = d_normed + jnp.dot(du[...], wt[1, :, at], preferred_element_type=F32)
        scaled = d_normed * gain_ref[:, at]
        grad = up[:, at].astype(F32) + scale * (scaled - wide * scale * scale * along[:, :1])
        up[:, at] = grad.astype(BF16)
        cp = pltpu.make_async_copy(up.at[:, at], gi_any.at[:, at], ls.at[3 + 2 * t])
        cp.start()
        stores.append(cp)

    table = {"a1": a1, "a2": a2, "a3": a3, "a4": a4, "a5": a5, "a6": a6,
             "b1": b1, "b2": b2, "b3": b3, "b4": b4, "b5": b5, "b6": b6}
    for line in ORDER:
        for task in line.split():
            kind, j = task.split(".")
            if kind == "f":
                f(int(j))
            else:
                table[kind](int(j), CHUNK[kind[0], int(j)])

    for cp in stores:
        cp.wait()
    for name in live:
        if name not in waited:
            sent(name)


N_COPIES = N_A * (2 + 4 + 4 + 4 + 4 + 2) + N_B * (2 + 2 + 8 + 2 + 2 + 2)


def solution(mesh):
    n_blk = mesh.shape["blk"]

    def local(inputs, upstream, norm_gain, gate_weight, up_weight, down_weight):
        tok, width = inputs.shape
        sh, ff = gate_weight.shape
        ch = ff // N_CHUNK
        own = jnp.stack([gate_weight.T, up_weight.T, down_weight.T])
        hbm = pl.BlockSpec(memory_space=pltpu.HBM)
        vmem = pl.BlockSpec(memory_space=pltpu.VMEM)
        flops = 9 * 2 * tok * width * ff
        lo, gi, g = pl.pallas_call(
            functools.partial(kernel, n_blk),
            name="ring",
            out_shape=(
                jax.ShapeDtypeStruct((tok, width), BF16),
                jax.ShapeDtypeStruct((tok, width), BF16),
                jax.ShapeDtypeStruct((3, ff, sh), BF16),
            ),
            in_specs=[hbm, hbm, vmem, hbm],
            out_specs=(hbm, hbm, vmem),
            scratch_shapes=[
                pltpu.VMEM((tok, width), BF16),
                pltpu.VMEM((tok, width), BF16),
                pltpu.VMEM((tok, width), BF16),
                pltpu.VMEM((tok, 128), F32),
                pltpu.VMEM((3, ff, width), BF16),
                pltpu.VMEM((SLOTS, 3, ch, width), BF16),
                pltpu.VMEM((N_B, 3, 3, ch, sh), BF16),
                pltpu.VMEM((N_A, 2, 2, 3, ch // 2, sh), BF16),
                pltpu.VMEM((N_A, 2, 2, 3, ch, sh), BF16),
                pltpu.VMEM((N_A, 2, 3, ch, sh), BF16),
                pltpu.VMEM((N_B, 2, 3, ch, 4 * sh), BF16),
                pltpu.VMEM((N_B, 2, 3, ch // 2, sh), BF16),
                pltpu.VMEM((N_B, 2, 3, ch, sh), BF16),
                pltpu.VMEM((ff, tok), BF16),
                pltpu.VMEM((ff, tok), BF16),
                pltpu.VMEM((ff, tok), BF16),
                pltpu.VMEM((tok, ff), BF16),
                pltpu.VMEM((tok, ff), BF16),
                pltpu.VMEM((tok, ff), BF16),
                pltpu.VMEM((128, tok), F32),
                pltpu.VMEM((tok, 128), F32),
                pltpu.SemaphoreType.DMA((N_COPIES,)),
                pltpu.SemaphoreType.DMA((N_COPIES,)),
                pltpu.SemaphoreType.DMA((18,)),
            ],
            compiler_params=pltpu.CompilerParams(
                collective_id=0, has_side_effects=True, vmem_limit_bytes=63 * 2**20
            ),
            cost_estimate=pl.CostEstimate(
                flops=flops, bytes_accessed=8 * tok * width, transcendentals=tok * ff
            ),
        )(inputs, upstream, norm_gain.reshape(1, width), own)
        return (lo, gi, g[0].T, g[1].T, g[2].T)

    tokens, weights = P(("blk", "dp"), None), P("dp", "blk")
    return jax.shard_map(
        local,
        mesh=mesh,
        in_specs=(tokens, tokens, P(), weights, weights, weights),
        out_specs=(tokens, tokens, weights, weights, weights),
        check_vma=False,
    )
```

time: 564 us -> 229 us (0.41)
  waiting for transfers between devices: 442 us -> 0 us
  Pallas kernels: 0 us -> 216 us
  matrix products: 53.3 us -> 0 us
  local copies, waits for them, and re-layouts: 32.4 us -> 9.01 us
  between operations: 14.2 us -> 0.64 us
  starting transfers between devices: 12.3 us -> 0 us
  other arithmetic: 8.88 us -> 2.82 us
    unnamed x9 -> x0, waiting for transfers between devices: 226 us -> none
    pallas_call x0 -> x1, Pallas kernels: none -> 216 us  [local(): pl.pallas_call(functools.partial(kernel, n_blk), name='ring', out_shape=(...]
    all_gather x3 -> x0, waiting for transfers between devices: 189 us -> none  [the longest x1 69.2 us: local(): lax.all_gather(moved_up, 'dp', axis=0, tiled=True)]
    dot_general x9 -> x0, matrix products: 53.3 us -> none  [the longest x3 18.6 us: contract_first(): lax.dot_general(left_rows, right_rows, (((0,), (0,)), ((), ())), preferre...]
    ppermute x6 -> x0, waiting for transfers between devices: 27.2 us -> none  [shifted(): lax.ppermute(value, axis, [(i, (i + by) % size) for i in range(size)])]
    unnamed x25 -> x4, local copies, waits for them, and re-layouts: 32.4 us -> 6.36 us
    ppermute x6 -> x0, starting transfers between devices: 11.9 us -> none  [shifted(): lax.ppermute(value, axis, [(i, (i + by) % size) for i in range(size)])]
    convert_element_type x1 -> x0, other arithmetic: 5.9 us -> none  [block_pass(): grad_rows = (rows_cot.astype(jnp.float32) + inv_rms * (scaled_grad - wide...]
  transfers between devices with their start and end apart: 12 -> 0, of which waited for: 10 -> 0; matrix products, arithmetic and copies ran while one was open for 13% -> 0% of each run, Pallas kernels for 0% -> 0%
where the time goes in v2:
time: 229 us; the launch traced here: 228 us
  Pallas kernels  216 us (94%)
  local copies, waits for them, and re-layouts  9.01 us (4%)
  other arithmetic  2.82 us (1%)
    pallas_call x1, Pallas kernels, local(): pl.pallas_call(functools.partial(kernel, n_blk), name='ring', out_shape=(...  216 us
    unnamed x4, local copies, waits for them, and re-layouts  6.36 us

profile of v2, /device:TPU:1, one launch (start us, length us, event | category | flops | bytes accessed | tf_op | source)
XLA Modules:
  0.0 228.0 jit_solution(1180138943839335296)
XLA Ops:
  0.6 2.8 %pad_maximum_fusion.own = bf16[3,448,640]{2,1,0:T(8,128)(2,1)} fusion(bf16[1,448,640]{2,1,0:T(8,128)(2,1)} %bitcast.22, bf16[1,448,640]{2,1,0:T(8,128)(2,1)} %bitcast.23, bf16[1,448,640]{2,1,0:T(8,128)(2,1)} %bitcast.24), kind=kLoop, calls=%fused_computation | loop fusion | flops 1720320 | bytes 3440640 | tf_op jit(solution)/shard_map/stack | solution.py:303
  3.4 215.5 %ring.1 = (bf16[384,5120]{1,0:T(8,128)(2,1)}, bf16[384,5120]{1,0:T(8,128)(2,1)}, bf16[3,448,640]{2,1,0:T(8,128)(2,1)}) custom-call(bf16[384,5120]{1,0:T(8,128)(2,1)} %x_any.1, bf16[384,5120]{1,0:T(8,128)(2,1)} %up_any.1, f32[1,5120]{1,0:T(1,128)} %bitcast.25, bf16[3,448,640]{2,1,0:T(8,128)(2,1)} %pad_maximum_fusion.own), custom_call_target="tpu_custom_call" | custom-call | flops 15854469120 | bytes 15728640 | tf_op jit(solution)/shard_map/ring/pallas_call | solution.py:307
  219.0 2.6 %slice_bitcast_fusion = (bf16[640,448]{0,1:T(8,128)(2,1)}, bf16[640,448]{0,1:T(8,128)(2,1)}, bf16[640,448]{0,1:T(8,128)(2,1)}) fusion(bf16[3,448,640]{2,1,0:T(8,128)(2,1)} %get-tuple-element.10), kind=kLoop, calls=%fused_computation.1 | loop fusion | bytes 3440640 | tf_op jit(solution)/shard_map/transpose | solution.py:350
  221.6 0.0 copy-start
  221.6 4.4 %copy.13 = bf16[384,5120]{1,0:T(8,128)(2,1)} copy(bf16[384,5120]{1,0:T(8,128)(2,1)} %get-tuple-element.19) | data formatting | bytes 7864320
  226.1 0.0 copy-done
  226.1 1.9 copy.14
Async XLA Ops:
  221.6 4.4 %copy-start = (bf16[384,5120]{1,0:T(8,128)(2,1)S(1)}, bf16[384,5120]{1,0:T(8,128)(2,1)}, u32[]{:S(2)}) copy-start(bf16[384,5120]{1,0:T(8,128)(2,1)} %get-tuple-element.20) | copy-start | bytes 11796484

commit v3 on v2

--- a/solution.py
+++ b/solution.py
@@ -13,12 +13,12 @@
 
 CHUNK = {("a", 0): 0, ("b", 0): 1, ("a", 1): 2, ("b", 1): 3, ("a", 2): 4, ("b", 2): 5, ("a", 3): 6}
 N_A, N_B, N_CHUNK = 4, 3, 7
-SLOTS = 4
+SLOTS = 5
 ORDER = (
     "a1.0 b1.0 b1.1 a1.1", "b1.2 a1.2 a2.0 b2.0", "b2.1 a1.3 a2.1 b2.2", "a2.2 a3.0 a2.3 b3.0",
-    "a3.1 b3.1 a4.0 a4.1", "b3.2 b4.0 a5.0 a5.1", "b5.0 b4.1 b6.0 b5.1", "b6.1 b4.2 a3.2 b5.2",
-    "a3.3 a6.0 a6.1 a4.2", "f.0 f.1 f.2 b6.2", "f.3 f.4 f.5 a4.3", "f.6 f.7 a5.2 a6.2",
-    "a5.3 a6.3",
+    "a3.1 b3.1 a4.0 a3.2", "a4.1 a3.3 b4.0 a5.0", "a4.2 a5.1 b4.1 a4.3", "b3.2 b5.0 a6.0 a6.1",
+    "f.0 f.1 f.2 a5.2", "f.3 b5.1 f.4 f.5", "f.6 f.7 a5.3 b4.2", "b6.0 a6.2 b6.1 b5.2",
+    "a6.3 b6.2",
 )
 
 

time: 229 us -> 200 us (0.87)
  Pallas kernels: 216 us -> 185 us
    pallas_call x1, Pallas kernels: 216 us -> 185 us  [local(): pl.pallas_call(functools.partial(kernel, n_blk), name='ring', out_shape=(...]
where the time goes in v3:
time: 200 us; the launch traced here: 197 us
  Pallas kernels  185 us (92%)
  local copies, waits for them, and re-layouts  9.01 us (5%)
  other arithmetic  2.82 us (1%)
    pallas_call x1, Pallas kernels, local(): pl.pallas_call(functools.partial(kernel, n_blk), name='ring', out_shape=(...  185 us
    unnamed x4, local copies, waits for them, and re-layouts  6.36 us

profile of v3, /device:TPU:1, one launch (start us, length us, event | category | flops | bytes accessed | tf_op | source)
XLA Modules:
  0.0 197.0 jit_solution(5819594794851295962)
XLA Ops:
  0.6 2.8 %pad_maximum_fusion.own = bf16[3,448,640]{2,1,0:T(8,128)(2,1)} fusion(bf16[1,448,640]{2,1,0:T(8,128)(2,1)} %bitcast.22, bf16[1,448,640]{2,1,0:T(8,128)(2,1)} %bitcast.23, bf16[1,448,640]{2,1,0:T(8,128)(2,1)} %bitcast.24), kind=kLoop, calls=%fused_computation | loop fusion | flops 1720320 | bytes 3440640 | tf_op jit(solution)/shard_map/stack | solution.py:303
  3.4 184.5 %ring.1 = (bf16[384,5120]{1,0:T(8,128)(2,1)}, bf16[384,5120]{1,0:T(8,128)(2,1)}, bf16[3,448,640]{2,1,0:T(8,128)(2,1)}) custom-call(bf16[384,5120]{1,0:T(8,128)(2,1)} %x_any.1, bf16[384,5120]{1,0:T(8,128)(2,1)} %up_any.1, f32[1,5120]{1,0:T(1,128)} %bitcast.25, bf16[3,448,640]{2,1,0:T(8,128)(2,1)} %pad_maximum_fusion.own), custom_call_target="tpu_custom_call" | custom-call | flops 15854469120 | bytes 15728640 | tf_op jit(solution)/shard_map/ring/pallas_call | solution.py:307
  188.0 2.6 %slice_bitcast_fusion = (bf16[640,448]{0,1:T(8,128)(2,1)}, bf16[640,448]{0,1:T(8,128)(2,1)}, bf16[640,448]{0,1:T(8,128)(2,1)}) fusion(bf16[3,448,640]{2,1,0:T(8,128)(2,1)} %get-tuple-element.10), kind=kLoop, calls=%fused_computation.1 | loop fusion | bytes 3440640 | tf_op jit(solution)/shard_map/transpose | solution.py:350
  190.6 0.0 copy-start
  190.6 4.4 %copy.13 = bf16[384,5120]{1,0:T(8,128)(2,1)} copy(bf16[384,5120]{1,0:T(8,128)(2,1)} %get-tuple-element.19) | data formatting | bytes 7864320
  195.1 0.0 copy-done
  195.1 1.9 copy.14
Async XLA Ops:
  190.6 4.4 %copy-start = (bf16[384,5120]{1,0:T(8,128)(2,1)S(1)}, bf16[384,5120]{1,0:T(8,128)(2,1)}, u32[]{:S(2)}) copy-start(bf16[384,5120]{1,0:T(8,128)(2,1)} %get-tuple-element.20) | copy-start | bytes 11796484
